TPU v7x, 32 devices: a whole 2x2x4 slice. The times are simulated.
32 devices in a mesh: tile: 8 (over z, x), row: 4 (over y, core).
Axes of the slice: x: 2, y: 2, z: 4, core: 2. Of those that a mesh axis runs over, the one named last changes fastest.
Arguments:
- amplitudes: float32 [576, 64, 256], P('tile'), may hold values from -6 to 6
- integrals: float32 [4, 512, 128, 256], P('row', 'tile'), may hold values from -0.125 to 0.125
- slot_ab: int32 [4, 512], P('row', 'tile'), may hold values from 0 to 17
- slot_cd: int32 [4, 512], P('row', 'tile'), may hold values from 0 to 575, as said below
- live_count: int32 [4, 8], P('row', 'tile'), may hold values from 1 to 64, as said below
- pair_list: int32 [64, 2], replicated, may hold values from 0 to 127, as said below
Outputs:
- symmetrized: float32 [64, 96, 96], P('tile', 'row')
Inputs may be any that keep to these rules, and one draw needn't show every extreme that they name: `slot_cd`: slot s of row index r belongs to tile index k = s // 64; its cd tile is held in amplitudes by tile index k - 1, k or k + 1, taken cyclically over the tile axis (cd tile c is held by tile index c // 72). `live_count`: slots at or after a device's count are unused. In every row index some device uses all 64 slots. `pair_list`: the rows are distinct pairs (i, j) with i != j, and for every row the reversed pair (j, i) is also a row.
All inputs are finite; a program needn't handle non-finite values.
Results may differ from a plain program's by a relative error of at most 0.0003.
Values sent between devices are 32-bit elements; how exact they have to be, the bound alone decides.
A program may use at most 64 MiB of HBM per device.

v0:
```python
import jax
import jax.numpy as jnp
from jax import lax
from jax.sharding import PartitionSpec as P

TS = 16
ATS = 8
SLAB = 96


def padded(x, sides, width):
    for axis, dim in sides:
        size, length = (lax.axis_size(axis), x.shape[dim])
        up = [(i, (i + 1) % size) for i in range(size)]
        down = [(j, i) for i, j in up]
        last = lax.slice_in_dim(x, length - width, length, axis=dim)
        first = lax.slice_in_dim(x, 0, width, axis=dim)
        before = lax.ppermute(last, axis, up)
        after = lax.ppermute(first, axis, down)
        x = jnp.concatenate([before, x, after], axis=dim)
    return x


def find_mirror(pair_list):
    first_orb = pair_list[:, 0]
    second = pair_list[:, 1]
    matches = (first_orb[:, None] == second[None, :]) & (second[:, None] == first_orb[None, :])
    columns = jnp.arange(pair_list.shape[0], dtype=jnp.int32)
    return jnp.sum(jnp.where(matches, columns[None, :], 0), axis=1)


def to_grid(totals, a_tiles, b_tiles):
    pair_count = totals.shape[1]
    shaped = totals.reshape(a_tiles, b_tiles, pair_count, ATS, TS)
    return jnp.transpose(shaped, (2, 0, 3, 1, 4)).reshape(pair_count, a_tiles * ATS, b_tiles * TS)


def shards(amplitudes, integrals, slot_ab, slot_cd, live_count, pair_list):
    highest = lax.Precision.HIGHEST
    tile_size = lax.axis_size("tile")
    row_size = lax.axis_size("row")
    tile_index = lax.axis_index("tile")
    shard_tiles = amplitudes.shape[0]
    pair_count = amplitudes.shape[1]
    extended = padded(amplitudes, (("tile", 0),), shard_tiles)
    blocks_all = integrals[0]
    ab_local = slot_ab[0]
    cd_global = slot_cd[0]
    owner_tile = cd_global // shard_tiles
    offset = (owner_tile - tile_index + 1 + tile_size) % tile_size
    ext_index = offset * shard_tiles + cd_global % shard_tiles
    live_total = live_count[0, 0]
    a_tiles = SLAB // (row_size * ATS)
    b_tiles = SLAB // TS
    tiles_ab = a_tiles * b_tiles
    block_width = integrals.shape[2]
    group_size = 8

    def block_step(block_index, totals):
        first_slot = block_index * group_size
        picked = lax.dynamic_slice_in_dim(ext_index, first_slot, group_size)
        ab_tiles = lax.dynamic_slice_in_dim(ab_local, first_slot, group_size)
        blocks = lax.dynamic_slice_in_dim(blocks_all, first_slot, group_size, 0)
        live_mask = (first_slot + jnp.arange(group_size, dtype=jnp.int32) < live_total).astype(
            jnp.float32
        )
        amp_tiles = jnp.take(extended, picked, axis=0)
        products = jnp.einsum(
            "spw,sbw->spb", amp_tiles, blocks, precision=highest, preferred_element_type=jnp.float32
        )
        one_hot = (ab_tiles[:, None] == jnp.arange(tiles_ab, dtype=jnp.int32)[None, :]).astype(
            jnp.float32
        ) * live_mask[:, None]
        return totals + jnp.einsum(
            "se,spb->epb", one_hot, products, precision=highest, preferred_element_type=jnp.float32
        )

    turn_count = (live_total + group_size - 1) // group_size
    start_totals = jnp.zeros((tiles_ab, pair_count, block_width), jnp.float32)
    totals = lax.fori_loop(0, turn_count, block_step, start_totals)
    whole_term = to_grid(totals, a_tiles, b_tiles)
    mirror = find_mirror(pair_list)
    reduced = lax.psum_scatter(whole_term, "tile", scatter_dimension=0, tiled=True)
    exchanged = lax.all_to_all(reduced, "row", split_axis=2, concat_axis=1, tiled=True)
    turned = jnp.transpose(exchanged, (0, 2, 1))
    everyone = lax.all_gather(turned, "tile", axis=0, tiled=True)
    local_pairs = reduced.shape[0]
    wanted = lax.dynamic_slice_in_dim(mirror, tile_index * local_pairs, local_pairs)
    return reduced + jnp.take(everyone, wanted, axis=0)


def solution(mesh):
    return jax.shard_map(
        shards,
        mesh=mesh,
        in_specs=(
            P("tile", None, None),
            P("row", "tile", None, None),
            P("row", "tile"),
            P("row", "tile"),
            P("row", "tile"),
            P(),
        ),
        out_specs=P("tile", "row", None),
        check_vma=False,
    )
```

profile of v0, /device:TPU:0, one launch (start us, length us, event | category | flops | bytes accessed | tf_op | source)
XLA Modules:
  0.0 421.5 jit_solution(5124547319537156772)
XLA Ops:
  6.5 2.9 collective-permute-start
  9.5 3.0 collective-permute-start.1
  13.9 198.1 %collective-permute-done = f32[72,64,256]{2,1,0:T(8,128)} collective-permute-done((f32[72,64,256]{2,1,0:T(8,128)}, f32[72,64,256]{2,1,0:T(8,128)}, u32[]{:S(2)}, u32[]{:S(2)}) %collective-permute-start) | collective-permute-done | bytes 4718624 | tf_op jit(solution)/shard_map/ppermute | solution.py:18
  212.0 2.2 collective-permute-done.1
  214.2 10.3 %pad_maximum_fusion = f32[216,64,256]{2,1,0:T(8,128)} fusion(f32[72,64,256]{2,1,0:T(8,128)} %collective-permute-done.1, f32[72,64,256]{2,1,0:T(8,128)} %param.8, f32[72,64,256]{2,1,0:T(8,128)} %collective-permute-done), kind=kLoop, calls=%fused_computation.22 | loop fusion | flops 7077888 | bytes 28311552 | tf_op jit(solution)/shard_map/concatenate | solution.py:20
  224.6 39.9 %while.10 = (s32[]{:T(128)}, f32[18,64,128]{2,0,1:T(8,128)S(1)}, s32[]{:T(128)}, s32[64]{0:T(128)S(1)}, s32[]{:T(128)}, /*index=5*/s32[64]{0:T(128)S(1)}, f32[21...) while((s32[]{:T(128)}, f32[18,64,128]{2,0,1:T(8,128)S(1)}, ...), condition=%wide.region_1.2_spmd, body=%wide.region_0.1_spmd.sunk | while | flops 215762288 | bytes 4329959 | solution.py:80
  225.3 5.6 %gather_fusion = f32[8,64,256]{2,1,0:T(8,128)S(1)} fusion(f32[216,64,256]{2,1,0:T(8,128)} %get-tuple-element.158, s32[1024]{0:T(1024)S(1)} %pad_clamp_fusion.3), kind=kCustom, calls=%fused_computation.clone.1 | custom fusion | bytes 1048608 | tf_op jit(solution)/shard_map/while/body/jit(_take)/gather | solution.py:67
  230.9 2.5 fusion.27
  233.5 1.0 convolution_add_fusion.2
  235.3 5.6 %gather_fusion = f32[8,64,256]{2,1,0:T(8,128)S(1)} fusion(f32[216,64,256]{2,1,0:T(8,128)} %get-tuple-element.158, s32[1024]{0:T(1024)S(1)} %pad_clamp_fusion.3), kind=kCustom, calls=%fused_computation.clone.1 | custom fusion | bytes 1048608 | tf_op jit(solution)/shard_map/while/body/jit(_take)/gather | solution.py:67
  240.9 2.5 fusion.27
  245.3 5.6 %gather_fusion = f32[8,64,256]{2,1,0:T(8,128)S(1)} fusion(f32[216,64,256]{2,1,0:T(8,128)} %get-tuple-element.158, s32[1024]{0:T(1024)S(1)} %pad_clamp_fusion.3), kind=kCustom, calls=%fused_computation.clone.1 | custom fusion | bytes 1048608 | tf_op jit(solution)/shard_map/while/body/jit(_take)/gather | solution.py:67
  250.9 2.5 fusion.27
  253.5 1.0 convolution_add_fusion.2
  255.3 5.6 %gather_fusion = f32[8,64,256]{2,1,0:T(8,128)S(1)} fusion(f32[216,64,256]{2,1,0:T(8,128)} %get-tuple-element.158, s32[1024]{0:T(1024)S(1)} %pad_clamp_fusion.3), kind=kCustom, calls=%fused_computation.clone.1 | custom fusion | bytes 1048608 | tf_op jit(solution)/shard_map/while/body/jit(_take)/gather | solution.py:67
  260.9 2.5 fusion.27
  263.5 1.0 convolution_add_fusion.2
  265.0 1.3 copy.21
  266.6 102.3 %reduce-scatter.2.cloned.1.call-done = f32[8,24,96]{2,1,0:T(8,128)} async-done(((f32[64,24,96]{2,1,0:T(8,128)}), f32[8,24,96]{2,1,0:T(8,128)}) %reduce-scatter.2.cloned.1.call-update) | async-done | bytes 73744 | tf_op jit(solution)/shard_map/reduce_scatter | solution.py:83
  368.9 1.1 copy.22
  370.9 3.3 all-to-all-start
  374.2 4.1 all-to-all-done
  380.4 32.1 %all_gather.3 = f32[64,24,96]{2,1,0:T(8,128)S(1)} all-gather(f32[8,24,96]{2,1,0:T(8,128)S(1)} %bitcast.47), channel_id=1, replica_groups=mesh['tile'=8,'row'=4] {'tile'}, dimensions={0}, use_global_device_ids=true | all-gather | bytes 663552 | tf_op jit(solution)/shard_map/all_gather | solution.py:86
  413.0 1.6 select_add_fusion
  (34 shorter events, 9.3 us)
Async XLA Ops:
  6.5 362.3 %reduce-scatter.2.cloned.1.call-start = ((), (), s32[]{:S(2)}) async-start(), calls=%async_computation.2 | async-start | bytes 884736 | tf_op jit(solution)/shard_map/reduce_scatter | solution.py:83
  6.5 205.4 %collective-permute-start = (f32[72,64,256]{2,1,0:T(8,128)}, f32[72,64,256]{2,1,0:T(8,128)}, u32[]{:S(2)}, u32[]{:S(2)}) collective-permute-start(f32[72,64,256]{2,1,0:T(8,128)} %param.8), channel_id=1, source_target_pairs={{0,4},{4,8},{8,12},{12,16},{16,20},{20,24},{24,28},{28,0},{1,5},{5... | collective-permute-start | bytes 14155784 | tf_op jit(solution)/shard_map/ppermute | solution.py:18
  9.5 204.7 %collective-permute-start.1 = (f32[72,64,256]{2,1,0:T(8,128)}, f32[72,64,256]{2,1,0:T(8,128)}, u32[]{:S(2)}, u32[]{:S(2)}) collective-permute-start(f32[72,64,256]{2,1,0:T(8,128)} %param.8), channel_id=1, source_target_pairs={{4,0},{8,4},{12,8},{16,12},{20,16},{24,20},{28,24},{0,28},{5,1},{9... | collective-permute-start | bytes 14155784 | tf_op jit(solution)/shard_map/ppermute | solution.py:19
  13.9 210.7 %copy-start.1 = (s32[1,64]{1,0:T(1,128)S(1)}, s32[1,64]{1,0:T(1,128)}, u32[]{:S(2)}) copy-start(s32[1,64]{1,0:T(1,128)} %param.10) | copy-start | bytes 772
  224.6 41.8 %copy-start = (s32[64,2]{0,1:T(2,128)S(1)}, s32[64,2]{0,1:T(2,128)}, u32[]{:S(2)}) copy-start(s32[64,2]{0,1:T(2,128)} %param.13) | copy-start | bytes 1540
  370.9 7.4 %all-to-all-start = ((f32[4,1,4608]{2,1,0:T(1,128)}), f32[4,1,4608]{2,1,0:T(1,128)S(1)}, u32[]{:S(2)}, u32[]{:S(2)}) async-start(f32[4,1,4608]{2,1,0:T(1,128)} %reshape.53), calls=%async_computation.1 | async-start | bytes 147456 | tf_op jit(solution)/shard_map/all_to_all | solution.py:84
Sparse Core Ops, SparseCore 0:
  266.4 102.3 reduce-scatter.1
where the time goes:
time: 422 us; the launch traced here: 421 us
  waiting for transfers between devices  307 us (73%)
  blocking collectives  32.1 us (8%)
  local copies, waits for them, and re-layouts  28.4 us (7%)
  other arithmetic  16.6 us (4%)
  between operations  14.2 us (3%)
  matrix products  14.1 us (3%)
  starting transfers between devices  9.27 us (2%)
    ppermute x1, waiting for transfers between devices, padded(): before = lax.ppermute(last, axis, up)  198 us
    reduce_scatter x1, waiting for transfers between devices, shards(): lax.psum_scatter(whole_term, 'tile', scatter_dimension=0, tiled=True)  102 us
    all_gather x1, blocking collectives, shards(): everyone = lax.all_gather(turned, 'tile', axis=0, tiled=True)  32.1 us
    gather x4, local copies, waits for them, and re-layouts, block_step(): amp_tiles = jnp.take(extended, picked, axis=0)  22.4 us
    concatenate x1, other arithmetic, padded(): x = jnp.concatenate([before, x, after], axis=dim)  10.3 us
    dot_general x4, matrix products, block_step(): jnp.einsum('spw,sbw->spb', amp_tiles, blocks, precision=highest, preferre...  10.1 us
  transfers between devices with their start and end apart: 4, of which 4 were waited for; matrix products, arithmetic and copies ran while one was open for 0% of the time, Pallas kernels for 0%

commit v1 on v0

--- a/solution.py
+++ b/solution.py
@@ -1,6 +1,10 @@
+import functools
+
 import jax
 import jax.numpy as jnp
 from jax import lax
+from jax.experimental import pallas as pl
+from jax.experimental.pallas import tpu as pltpu
 from jax.sharding import PartitionSpec as P
 
 TS = 16
@@ -89,9 +93,321 @@
     return reduced + jnp.take(everyone, wanted, axis=0)
 
 
+MESH = pl.DeviceIdType.MESH
+CHUNK = 2
+GROUP = 4
+DEPTH = 3
+
+
+def place():
+    k = lax.axis_index("tile")
+    r = lax.axis_index("row")
+    return k, r, k // 2, k % 2
+
+
+def greet(devices):
+    barrier = pltpu.get_barrier_semaphore()
+    for device in devices:
+        pl.semaphore_signal(barrier, inc=1, device_id=device, device_id_type=MESH)
+    pl.semaphore_wait(barrier, len(devices))
+
+
+def halo_kernel(tiles, amp, halo, send, rx, rz, ry, rc):
+    k, r, z, x = place()
+    y, core = r // 2, r % 2
+    sixth = tiles // 6
+    half = sixth // CHUNK
+    count = 2 * half
+    other_x = (z * 2 + 1 - x, r)
+    up = ((z + 1) % 4 * 2 + x, r)
+    down = ((z + 3) % 4 * 2 + x, r)
+    next_z = (jnp.where(x == 0, up[0], down[0]), r)
+    other_y = (k, (1 - y) * 2 + core)
+    other_core = (k, y * 2 + 1 - core)
+    greet((other_x, up, down, other_y, other_core))
+
+    def first_of(yy, cc, j):
+        own = (yy * 2 + cc) * sixth + j * CHUNK
+        both = (4 + cc) * sixth + (j - half) * CHUNK
+        return own if j < half else both
+
+    def remote(src, dst, sent, received, device):
+        return pltpu.make_async_remote_copy(
+            src_ref=src, dst_ref=dst, send_sem=sent, recv_sem=received, device_id=device, device_id_type=MESH
+        )
+
+    def at(side, first):
+        return halo.at[side, pl.ds(first, CHUNK)]
+
+    def copy_x(j):
+        first = first_of(y, core, j)
+        return remote(amp.at[pl.ds(first, CHUNK)], at(0, first), send.at[0, j], rx.at[j], other_x)
+
+    def copy_z(j):
+        first = first_of(y, core, j)
+        return remote(at(0, first), at(1, first), send.at[1, j], rz.at[j], next_z)
+
+    def copy_y(side, j):
+        first = first_of(y, core, j)
+        return remote(at(side, first), at(side, first), send.at[2 + side, j], ry.at[side, j], other_y)
+
+    def copy_c(side, j):
+        first = first_of(y, core, j) if j < count else first_of(1 - y, core, j - count)
+        return remote(at(side, first), at(side, first), send.at[4 + side, j], rc.at[side, j], other_core)
+
+    sends = []
+
+    def go(copy):
+        copy.start()
+        sends.append(copy)
+
+    for j in range(count):
+        go(copy_x(j))
+    lag = 1
+    for i in range(count + 3 * lag):
+        if i < count:
+            copy_x(i).wait_recv()
+            go(copy_z(i))
+            if i < half:
+                go(copy_y(0, i))
+            go(copy_c(0, i))
+        j = i - lag
+        if 0 <= j < count:
+            copy_z(j).wait_recv()
+            if j < half:
+                go(copy_y(1, j))
+            go(copy_c(1, j))
+        j = i - 2 * lag
+        if 0 <= j < half:
+            copy_y(0, j).wait_recv()
+            go(copy_c(0, count + j))
+        j = i - 3 * lag
+        if 0 <= j < half:
+            copy_y(1, j).wait_recv()
+            go(copy_c(1, count + j))
+    for j in range(count + half):
+        for side in range(2):
+            copy_c(side, j).wait_recv()
+    for copy in sends:
+        copy.wait_send()
+
+
+def halo_of(amplitudes):
+    tiles = amplitudes.shape[0]
+    count = tiles // 3 // CHUNK
+    return pl.pallas_call(
+        functools.partial(halo_kernel, tiles),
+        out_shape=jax.ShapeDtypeStruct((2,) + amplitudes.shape, jnp.float32),
+        in_specs=[pl.BlockSpec(memory_space=pl.ANY)],
+        out_specs=pl.BlockSpec(memory_space=pl.ANY),
+        scratch_shapes=[
+            pltpu.SemaphoreType.DMA((6, count + count // 2)),
+            pltpu.SemaphoreType.DMA((count,)),
+            pltpu.SemaphoreType.DMA((count,)),
+            pltpu.SemaphoreType.DMA((2, count // 2)),
+            pltpu.SemaphoreType.DMA((2, count + count // 2)),
+        ],
+        compiler_params=pltpu.CompilerParams(collective_id=0, has_side_effects=True),
+    )(amplitudes)
+
+
+def split(v):
+    high = v.astype(jnp.bfloat16)
+    low = (v - high.astype(jnp.float32)).astype(jnp.bfloat16)
+    return jnp.concatenate([high, low], axis=0)
+
+
+def slots_kernel(amp, halo, blocks, ab, cd, live, pairs, out, abuf, bbuf, asem, bsem, table):
+    k = lax.axis_index("tile")
+    tiles = amp.shape[0]
+    pair_count = amp.shape[1]
+    width = blocks.shape[1]
+    groups = (live[0, 0] + GROUP - 1) // GROUP
+
+    def copies(s, slot, from_amp, from_halo):
+        c = cd[0, s]
+        owner = c // tiles
+        local = c - owner * tiles
+        side = jnp.where(owner == k // 2 * 2 + 1 - k % 2, 0, 1)
+        if from_amp:
+            return pltpu.make_async_copy(amp.at[local], abuf.at[slot], asem.at[slot])
+        if from_halo:
+            return pltpu.make_async_copy(halo.at[side, local], abuf.at[slot], asem.at[slot])
+        return pltpu.make_async_copy(blocks.at[s], bbuf.at[slot], bsem.at[slot])
+
+    def fetch(g):
+        @pl.when(g < groups)
+        def _():
+            for i in range(GROUP):
+                s = g * GROUP + i
+                slot = g % DEPTH * GROUP + i
+                own = cd[0, s] // tiles == k
+                pl.when(own)(lambda: copies(s, slot, True, False).start())
+                pl.when(jnp.logical_not(own))(lambda: copies(s, slot, False, True).start())
+                copies(s, slot, False, False).start()
+
+    for g in range(DEPTH - 1):
+        fetch(g)
+    out[...] = jnp.zeros_like(out)
+
+    def note(p, carry):
+        table[pairs[p, 0] * 128 + pairs[p, 1]] = p
+        return carry
+
+    lax.fori_loop(0, pair_count, note, 0)
+
+    def step(g, carry):
+        fetch(g + DEPTH - 1)
+        base = g % DEPTH * GROUP
+        for i in range(GROUP):
+            slot = base + i
+            pltpu.make_async_copy(amp.at[0], abuf.at[slot], asem.at[slot]).wait()
+            pltpu.make_async_copy(blocks.at[0], bbuf.at[slot], bsem.at[slot]).wait()
+        terms = []
+        for i in range(GROUP):
+            left = split(abuf[base + i])
+            right = split(bbuf[base + i])
+            full = lax.dot_general(
+                left, right, (((1,), (1,)), ((), ())), preferred_element_type=jnp.float32
+            )
+            top, low = full[:pair_count], full[pair_count:]
+            terms.append(top[:, :width] + (top[:, width:] + (low[:, :width] + low[:, width:])))
+        for i in range(GROUP):
+            s = g * GROUP + i
+            term = jnp.where(s < live[0, 0], terms[i], 0.0).reshape(out.shape[0], out.shape[3], width)
+            e = ab[0, s]
+            out[:, 0, e] += term
+        return carry
+
+    lax.fori_loop(0, groups, step, 0)
+
+    def turn(p, carry):
+        m = table[pairs[p, 1] * 128 + pairs[p, 0]]
+        out[p // 8, 1, :, pl.ds(p % 8, 1), :] = out[m // 8, 0, :, pl.ds(m % 8, 1), :]
+        return carry
+
+    lax.fori_loop(0, pair_count, turn, 0)
+
+
+def slot_sums(amplitudes, halo, blocks, ab, cd, live, pair_list, tiles_ab):
+    pair_count, depth = amplitudes.shape[1:]
+    width = blocks.shape[1]
+    anywhere = pl.BlockSpec(memory_space=pl.ANY)
+    scalars = pl.BlockSpec(memory_space=pltpu.SMEM)
+    return pl.pallas_call(
+        slots_kernel,
+        out_shape=jax.ShapeDtypeStruct((pair_count // 8, 2, tiles_ab, 8, width), jnp.float32),
+        in_specs=[anywhere] * 3 + [scalars] * 4,
+        out_specs=pl.BlockSpec(memory_space=pltpu.VMEM),
+        scratch_shapes=[
+            pltpu.VMEM((DEPTH * GROUP, pair_count, depth), jnp.float32),
+            pltpu.VMEM((DEPTH * GROUP, width, depth), jnp.float32),
+            pltpu.SemaphoreType.DMA((DEPTH * GROUP,)),
+            pltpu.SemaphoreType.DMA((DEPTH * GROUP,)),
+            pltpu.SMEM((128 * 128,), jnp.int32),
+        ],
+        compiler_params=pltpu.CompilerParams(vmem_limit_bytes=32 * 1024 * 1024),
+    )(amplitudes, halo, blocks, ab, cd, live, pair_list)
+
+
+def sum_kernel(sums, ladder, turned, bx, sz, bz, mine, send_x, recv_x, send_z, recv_z, send_r, recv_r):
+    k, r, z, x = place()
+    other_x = (z * 2 + 1 - x, r)
+    zs = [((z + i) % 4 * 2 + x, r) for i in range(1, 4)]
+    rows = [(k, (r + i) % 4) for i in range(1, 4)]
+    greet([other_x] + zs + rows)
+
+    def remote(src, dst, sent, received, device):
+        return pltpu.make_async_remote_copy(
+            src_ref=src, dst_ref=dst, send_sem=sent, recv_sem=received, device_id=device, device_id_type=MESH
+        )
+
+    order = (2, 1, 3, 0)
+    over_x = [remote(sums.at[(z + i) % 4 * 2 + 1 - x], bx.at[i], send_x.at[i], recv_x.at[i], other_x) for i in range(4)]
+    over_z = [None] + [remote(sz.at[i], bz.at[i], send_z.at[i], recv_z.at[i], zs[i - 1]) for i in range(1, 4)]
+    for i in order:
+        over_x[i].start()
+    for i in order:
+        over_x[i].wait_recv()
+        total = bx[i] + sums[(z + i) % 4 * 2 + x]
+        if i > 0:
+            sz[i] = total
+            over_z[i].start()
+        else:
+            mine[...] = total
+    for i in (1, 3, 2):
+        over_z[i].wait_recv()
+    total = mine[...] + bz[1] + bz[2] + bz[3]
+    ladder[...] = total[0].reshape(ladder.shape)
+    mine[...] = total
+    parts = mine.at[1]
+
+    def over_row(i):
+        first = (r + i) % 4 * 3 // 2
+        return [
+            remote(
+                parts.at[pl.ds(t * 6 + first, 2)], turned.at[r, t], send_r.at[i, t], recv_r.at[i, t], rows[i - 1]
+            )
+            for t in range(3)
+        ]
+
+    copies = [c for i in range(1, 4) for c in over_row(i)]
+    for c in copies:
+        c.start()
+    own = r * 3 // 2
+    for t in range(3):
+        turned[r, t] = mine[1, pl.ds(t * 6 + own, 2)]
+    for i in range(1, 4):
+        source = (r + 4 - i) % 4
+        for t in range(3):
+            remote(
+                parts.at[pl.ds(0, 2)], turned.at[source, t], send_r.at[i, t], recv_r.at[i, t], rows[i - 1]
+            ).wait_recv()
+    for c in copies + over_x + over_z[1:]:
+        c.wait_send()
+
+
+def sum_over_tile(sums):
+    chunk = sums.shape[1:]
+    vmem = pl.BlockSpec(memory_space=pltpu.VMEM)
+    dma = pltpu.SemaphoreType.DMA
+    return pl.pallas_call(
+        sum_kernel,
+        out_shape=(
+            jax.ShapeDtypeStruct((3, 6) + chunk[2:], jnp.float32),
+            jax.ShapeDtypeStruct((4, 3, 2) + chunk[2:], jnp.float32),
+        ),
+        in_specs=[vmem],
+        out_specs=(vmem, vmem),
+        scratch_shapes=[
+            pltpu.VMEM((4,) + chunk, jnp.float32),
+            pltpu.VMEM((4,) + chunk, jnp.float32),
+            pltpu.VMEM((4,) + chunk, jnp.float32),
+            pltpu.VMEM(chunk, jnp.float32),
+            dma((4,)), dma((4,)), dma((4,)), dma((4,)), dma((4, 3)), dma((4, 3)),
+        ],
+        compiler_params=pltpu.CompilerParams(
+            collective_id=1, has_side_effects=True, vmem_limit_bytes=32 * 1024 * 1024
+        ),
+    )(sums)
+
+
+def shards_8x4(amplitudes, integrals, slot_ab, slot_cd, live_count, pair_list):
+    halo = halo_of(amplitudes)
+    sums = slot_sums(amplitudes, halo, integrals[0], slot_ab, slot_cd, live_count, pair_list, 18)
+    ladder, turned = sum_over_tile(sums)
+    local_pairs = ladder.shape[2]
+    grid = jnp.transpose(ladder.reshape(3, 6, local_pairs, ATS, TS), (2, 0, 3, 1, 4)).reshape(local_pairs, 24, SLAB)
+    other = turned.reshape(4, 3, 2, local_pairs, ATS, TS)
+    other = jnp.transpose(other, (3, 2, 5, 0, 1, 4)).reshape(local_pairs, 2 * TS, SLAB)
+    shift = lax.axis_index("row") % 2 * 8
+    return grid + lax.dynamic_slice_in_dim(other, shift, 24, axis=1)
+
+
 def solution(mesh):
+    fast = mesh.shape["tile"] == 8 and mesh.shape["row"] == 4
     return jax.shard_map(
-        shards,
+        shards_8x4 if fast else shards,
         mesh=mesh,
         in_specs=(
             P("tile", None, None),

time: 422 us -> 118 us (0.28)
  waiting for transfers between devices: 307 us -> 0 us
  Pallas kernels: 0 us -> 109 us
  blocking collectives: 32.1 us -> 0 us
  local copies, waits for them, and re-layouts: 28.4 us -> 8.17 us
  other arithmetic: 16.6 us -> 0.66 us
  matrix products: 14.1 us -> 0 us
  between operations: 14.2 us -> 0.77 us
  starting transfers between devices: 9.27 us -> 0 us
    ppermute x2 -> x0, waiting for transfers between devices: 200 us -> none  [the longest x1 198 us: padded(): before = lax.ppermute(last, axis, up)]
    pallas_call x0 -> x3, Pallas kernels: none -> 109 us  [the longest x1 61.2 us: halo_of(): pl.pallas_call(functools.partial(halo_kernel, tiles), out_shape=jax.Shape...]
    reduce_scatter x1 -> x0, waiting for transfers between devices: 102 us -> none  [shards(): lax.psum_scatter(whole_term, 'tile', scatter_dimension=0, tiled=True)]
    all_gather x1 -> x0, blocking collectives: 32.1 us -> none  [shards(): everyone = lax.all_gather(turned, 'tile', axis=0, tiled=True)]
    gather x5 -> x0, local copies, waits for them, and re-layouts: 23 us -> none  [the longest x4 22.4 us: block_step(): amp_tiles = jnp.take(extended, picked, axis=0)]
    dot_general x8 -> x0, matrix products: 14.1 us -> none  [the longest x4 10.1 us: block_step(): jnp.einsum('spw,sbw->spb', amp_tiles, blocks, precision=highest, preferre...]
    concatenate x1 -> x0, other arithmetic: 10.3 us -> none  [padded(): x = jnp.concatenate([before, x, after], axis=dim)]
    ppermute x2 -> x0, starting transfers between devices: 5.98 us -> none  [the longest x1 3.04 us: padded(): after = lax.ppermute(first, axis, down)]
  transfers between devices with their start and end apart: 4 -> 0, of which waited for: 4 -> 0; matrix products, arithmetic and copies ran while one was open for 0% -> 0% of each run, Pallas kernels for 0% -> 0%
where the time goes in v1:
time: 118 us; the launch traced here: 119 us
  Pallas kernels  109 us (92%)
  local copies, waits for them, and re-layouts  8.17 us (7%)
    pallas_call x1, Pallas kernels, halo_of(): pl.pallas_call(functools.partial(halo_kernel, tiles), out_shape=jax.Shape...  61.2 us
    pallas_call x1, Pallas kernels, sum_over_tile(): pl.pallas_call(sum_kernel, out_shape=(jax.ShapeDtypeStruct((3, 6) + chunk...  36.1 us
    pallas_call x1, Pallas kernels, slot_sums(): pl.pallas_call(slots_kernel, out_shape=jax.ShapeDtypeStruct((pair_count /...  11.8 us
    unnamed x12, local copies, waits for them, and re-layouts  5.97 us

profile of v1, /device:TPU:0, one launch (start us, length us, event | category | flops | bytes accessed | tf_op | source)
XLA Modules:
  0.0 118.7 jit_solution(8168850811562033290)
XLA Ops:
  0.0 0.0 copy-start.2
  0.0 0.0 copy-start.3
  0.0 0.0 copy-start.4
  0.0 61.2 %shard_map.64.halo = f32[2,72,64,256]{3,2,1,0:T(8,128)} custom-call(f32[72,64,256]{2,1,0:T(8,128)} %amp.3), custom_call_target="tpu_custom_call" | custom-call | tf_op jit(solution)/shard_map/pallas_call | solution.py:198
  61.8 0.0 copy-done.4
  61.8 0.1 copy.10.pairs
  61.9 0.0 copy-done.2
  61.9 0.0 copy-done.3
  61.9 0.0 copy-start
  62.0 2.3 %copy-done = f32[72,64,256]{2,1,0:T(8,128)S(1)} copy-done((f32[72,64,256]{2,1,0:T(8,128)S(1)}, f32[72,64,256]{2,1,0:T(8,128)}, u32[]{:S(2)}) %copy-start) | copy-done | bytes 4718616
  64.3 0.0 copy-start.1
  64.3 3.4 %copy-done.1 = f32[1,64,128,256]{3,2,1,0:T(8,128)S(1)} copy-done((f32[1,64,128,256]{3,2,1,0:T(8,128)S(1)}, f32[1,64,128,256]{3,2,1,0:T(8,128)}, u32[]{:S(2)}) %copy-start.1) | copy-done | bytes 8388632
  67.7 11.8 %shard_map.65.sums = f32[8,2,18,8,128]{4,3,2,1,0:T(8,128)S(1)} custom-call(f32[72,64,256]{2,1,0:T(8,128)S(1)} %copy-done, f32[2,72,64,256]{3,2,1,0:T(8,128)} %shard_map.64.halo, f32[64,128,256]{2,1,0:T(8,128)S(1)} %bitcast.13, s32[1,64]{1,0:T(1,128)S(1)} %copy-done.2, s32[1,64]{1,0:T(1,128)S(1)} %copy-done.3, s32[1,1]{1,0:T(1,128)S(6)} %copy.19.live, ...), custom_call_target="tpu_custom_call" | custom-call | tf_op jit(solution)/shard_map/pallas_call | solution.py:297
  79.4 36.1 %shard_map.66 = (f32[3,6,8,128]{3,2,1,0:T(8,128)S(1)}, f32[4,3,2,8,128]{4,3,2,1,0:T(8,128)S(1)}) custom-call(f32[8,2,18,8,128]{4,3,2,1,0:T(8,128)S(1)} %shard_map.65.sums), custom_call_target="tpu_custom_call" | custom-call | tf_op jit(solution)/shard_map/pallas_call | solution.py:374
  115.6 0.2 reshape.12
  115.8 0.4 copy.18
  116.2 0.2 reshape.13
  116.4 0.2 reshape.14
  116.6 0.6 copy.17
  117.2 0.4 reshape.15
  117.7 0.2 constant_dynamic-slice_fusion
  117.9 0.1 copy.14
  118.0 0.7 add.12
Async XLA Ops:
  0.0 61.9 %copy-start.2 = (s32[1,64]{1,0:T(1,128)S(1)}, s32[1,64]{1,0:T(1,128)}, u32[]{:S(2)}) copy-start(s32[1,64]{1,0:T(1,128)} %ab.1) | copy-start | bytes 772
  0.0 61.9 %copy-start.3 = (s32[1,64]{1,0:T(1,128)S(1)}, s32[1,64]{1,0:T(1,128)}, u32[]{:S(2)}) copy-start(s32[1,64]{1,0:T(1,128)} %cd.1) | copy-start | bytes 772
  0.0 61.8 %copy-start.4 = (s32[64,2]{0,1:T(2,128)S(1)}, s32[64,2]{0,1:T(2,128)}, u32[]{:S(2)}) copy-start(s32[64,2]{0,1:T(2,128)} %param.11) | copy-start | bytes 1540
  61.9 2.3 %copy-start = (f32[72,64,256]{2,1,0:T(8,128)S(1)}, f32[72,64,256]{2,1,0:T(8,128)}, u32[]{:S(2)}) copy-start(f32[72,64,256]{2,1,0:T(8,128)} %amp.3) | copy-start | bytes 14155780
  64.3 3.4 %copy-start.1 = (f32[1,64,128,256]{3,2,1,0:T(8,128)S(1)}, f32[1,64,128,256]{3,2,1,0:T(8,128)}, u32[]{:S(2)}) copy-start(f32[1,64,128,256]{3,2,1,0:T(8,128)} %param.7) | copy-start | bytes 25165828

commit v2 on v1

--- a/solution.py
+++ b/solution.py
@@ -95,8 +95,10 @@
 
 MESH = pl.DeviceIdType.MESH
 CHUNK = 2
-GROUP = 4
-DEPTH = 3
+WINDOW = 2
+GROUP = 8
+AHEAD = 2
+VMEM_BYTES = 56 * 1024 * 1024
 
 
 def place():
@@ -112,7 +114,7 @@
     pl.semaphore_wait(barrier, len(devices))
 
 
-def halo_kernel(tiles, amp, halo, send, rx, rz, ry, rc):
+def halo_kernel(tiles, amp, halo, send, rx, rz, ry, rc, own_sem):
     k, r, z, x = place()
     y, core = r // 2, r % 2
     sixth = tiles // 6
@@ -137,7 +139,7 @@
         )
 
     def at(side, first):
-        return halo.at[side, pl.ds(first, CHUNK)]
+        return halo.at[pl.ds(side * tiles + first, CHUNK)]
 
     def copy_x(j):
         first = first_of(y, core, j)
@@ -161,12 +163,16 @@
         copy.start()
         sends.append(copy)
 
-    for j in range(count):
+    for j in range(WINDOW):
         go(copy_x(j))
+    own = pltpu.make_async_copy(amp, halo.at[pl.ds(2 * tiles, tiles)], own_sem)
+    own.start()
     lag = 1
     for i in range(count + 3 * lag):
         if i < count:
             copy_x(i).wait_recv()
+            if i + WINDOW < count:
+                go(copy_x(i + WINDOW))
             go(copy_z(i))
             if i < half:
                 go(copy_y(0, i))
@@ -190,6 +196,7 @@
             copy_c(side, j).wait_recv()
     for copy in sends:
         copy.wait_send()
+    own.wait()
 
 
 def halo_of(amplitudes):
@@ -197,7 +204,7 @@
     count = tiles // 3 // CHUNK
     return pl.pallas_call(
         functools.partial(halo_kernel, tiles),
-        out_shape=jax.ShapeDtypeStruct((2,) + amplitudes.shape, jnp.float32),
+        out_shape=jax.ShapeDtypeStruct((3 * tiles,) + amplitudes.shape[1:], jnp.float32),
         in_specs=[pl.BlockSpec(memory_space=pl.ANY)],
         out_specs=pl.BlockSpec(memory_space=pl.ANY),
         scratch_shapes=[
@@ -206,8 +213,11 @@
             pltpu.SemaphoreType.DMA((count,)),
             pltpu.SemaphoreType.DMA((2, count // 2)),
             pltpu.SemaphoreType.DMA((2, count + count // 2)),
+            pltpu.SemaphoreType.DMA,
         ],
-        compiler_params=pltpu.CompilerParams(collective_id=0, has_side_effects=True),
+        compiler_params=pltpu.CompilerParams(
+            collective_id=0, has_side_effects=True, vmem_limit_bytes=VMEM_BYTES
+        ),
     )(amplitudes)
 
 
@@ -217,37 +227,39 @@
     return jnp.concatenate([high, low], axis=0)
 
 
-def slots_kernel(amp, halo, blocks, ab, cd, live, pairs, out, abuf, bbuf, asem, bsem, table):
+def slots_kernel(halo, blocks, ab, cd, live, pairs, out, abuf, bbuf, asem, bsem, table):
     k = lax.axis_index("tile")
-    tiles = amp.shape[0]
-    pair_count = amp.shape[1]
+    tiles = halo.shape[0] // 3
+    pair_count = halo.shape[1]
     width = blocks.shape[1]
     groups = (live[0, 0] + GROUP - 1) // GROUP
-
-    def copies(s, slot, from_amp, from_halo):
-        c = cd[0, s]
-        owner = c // tiles
-        local = c - owner * tiles
-        side = jnp.where(owner == k // 2 * 2 + 1 - k % 2, 0, 1)
-        if from_amp:
-            return pltpu.make_async_copy(amp.at[local], abuf.at[slot], asem.at[slot])
-        if from_halo:
-            return pltpu.make_async_copy(halo.at[side, local], abuf.at[slot], asem.at[slot])
-        return pltpu.make_async_copy(blocks.at[s], bbuf.at[slot], bsem.at[slot])
+    x = k % 2
+    other_x = k + 1 - 2 * x
+    next_z = lax.rem(k + 7 + 2 * x, 8)
+
+    def block_copy(g):
+        return pltpu.make_async_copy(
+            blocks.at[pl.ds(g * GROUP, GROUP)], bbuf.at[pl.ds(g * GROUP, GROUP)], bsem.at[g]
+        )
 
     def fetch(g):
-        @pl.when(g < groups)
-        def _():
-            for i in range(GROUP):
-                s = g * GROUP + i
-                slot = g % DEPTH * GROUP + i
-                own = cd[0, s] // tiles == k
-                pl.when(own)(lambda: copies(s, slot, True, False).start())
-                pl.when(jnp.logical_not(own))(lambda: copies(s, slot, False, True).start())
-                copies(s, slot, False, False).start()
-
-    for g in range(DEPTH - 1):
-        fetch(g)
+        for i in range(GROUP):
+            s = g * GROUP + i
+            c = cd[0, s]
+            mine = (c >= k * tiles) & (c < (k + 1) * tiles)
+            beside = (c >= other_x * tiles) & (c < (other_x + 1) * tiles)
+            shift = jnp.where(mine, 2 - k, jnp.where(beside, -other_x, 1 - next_z))
+            pltpu.make_async_copy(halo.at[c + shift * tiles], abuf.at[s], asem.at[g]).start()
+
+    def start_blocks(g, carry):
+        block_copy(g).start()
+        return carry
+
+    block_copy(0).start()
+    fetch(0)
+    lax.fori_loop(1, groups, start_blocks, 0)
+    for g in range(1, AHEAD):
+        pl.when(g < groups)(functools.partial(fetch, g))
     out[...] = jnp.zeros_like(out)
 
     def note(p, carry):
@@ -257,12 +269,12 @@
     lax.fori_loop(0, pair_count, note, 0)
 
     def step(g, carry):
-        fetch(g + DEPTH - 1)
-        base = g % DEPTH * GROUP
-        for i in range(GROUP):
-            slot = base + i
-            pltpu.make_async_copy(amp.at[0], abuf.at[slot], asem.at[slot]).wait()
-            pltpu.make_async_copy(blocks.at[0], bbuf.at[slot], bsem.at[slot]).wait()
+        base = g * GROUP
+        pl.when(g + AHEAD < groups)(lambda: fetch(g + AHEAD))
+        pltpu.make_async_copy(
+            halo.at[pl.ds(0, GROUP)], abuf.at[pl.ds(base, GROUP)], asem.at[g]
+        ).wait()
+        block_copy(g).wait()
         terms = []
         for i in range(GROUP):
             left = split(abuf[base + i])
@@ -289,25 +301,25 @@
     lax.fori_loop(0, pair_count, turn, 0)
 
 
-def slot_sums(amplitudes, halo, blocks, ab, cd, live, pair_list, tiles_ab):
-    pair_count, depth = amplitudes.shape[1:]
-    width = blocks.shape[1]
+def slot_sums(halo, blocks, ab, cd, live, pair_list, tiles_ab):
+    pair_count, depth = halo.shape[1:]
+    slots, width = blocks.shape[:2]
     anywhere = pl.BlockSpec(memory_space=pl.ANY)
     scalars = pl.BlockSpec(memory_space=pltpu.SMEM)
     return pl.pallas_call(
         slots_kernel,
         out_shape=jax.ShapeDtypeStruct((pair_count // 8, 2, tiles_ab, 8, width), jnp.float32),
-        in_specs=[anywhere] * 3 + [scalars] * 4,
+        in_specs=[anywhere] * 2 + [scalars] * 4,
         out_specs=pl.BlockSpec(memory_space=pltpu.VMEM),
         scratch_shapes=[
-            pltpu.VMEM((DEPTH * GROUP, pair_count, depth), jnp.float32),
-            pltpu.VMEM((DEPTH * GROUP, width, depth), jnp.float32),
-            pltpu.SemaphoreType.DMA((DEPTH * GROUP,)),
-            pltpu.SemaphoreType.DMA((DEPTH * GROUP,)),
+            pltpu.VMEM((slots, pair_count, depth), jnp.float32),
+            pltpu.VMEM((slots, width, depth), jnp.float32),
+            pltpu.SemaphoreType.DMA((slots // GROUP,)),
+            pltpu.SemaphoreType.DMA((slots // GROUP,)),
             pltpu.SMEM((128 * 128,), jnp.int32),
         ],
-        compiler_params=pltpu.CompilerParams(vmem_limit_bytes=32 * 1024 * 1024),
-    )(amplitudes, halo, blocks, ab, cd, live, pair_list)
+        compiler_params=pltpu.CompilerParams(vmem_limit_bytes=VMEM_BYTES),
+    )(halo, blocks, ab, cd, live, pair_list)
 
 
 def sum_kernel(sums, ladder, turned, bx, sz, bz, mine, send_x, recv_x, send_z, recv_z, send_r, recv_r):
@@ -322,21 +334,32 @@
             src_ref=src, dst_ref=dst, send_sem=sent, recv_sem=received, device_id=device, device_id_type=MESH
         )
 
-    order = (2, 1, 3, 0)
-    over_x = [remote(sums.at[(z + i) % 4 * 2 + 1 - x], bx.at[i], send_x.at[i], recv_x.at[i], other_x) for i in range(4)]
-    over_z = [None] + [remote(sz.at[i], bz.at[i], send_z.at[i], recv_z.at[i], zs[i - 1]) for i in range(1, 4)]
-    for i in order:
-        over_x[i].start()
-    for i in order:
-        over_x[i].wait_recv()
-        total = bx[i] + sums[(z + i) % 4 * 2 + x]
+    steps = [(i, h) for i in (2, 1, 3, 0) for h in range(2)]
+    over_x = {
+        (i, h): remote(
+            sums.at[(z + i) % 4 * 2 + 1 - x, h], bx.at[i, h], send_x.at[i, h], recv_x.at[i, h], other_x
+        )
+        for i, h in steps
+    }
+    over_z = {
+        (i, h): remote(sz.at[i, h], bz.at[i, h], send_z.at[i, h], recv_z.at[i, h], zs[i - 1])
+        for i, h in steps if i > 0
+    }
+    for step in steps[:WINDOW]:
+        over_x[step].start()
+    for j, (i, h) in enumerate(steps):
+        over_x[i, h].wait_recv()
+        if j + WINDOW < len(steps):
+            over_x[steps[j + WINDOW]].start()
+        total = bx[i, h] + sums[(z + i) % 4 * 2 + x, h]
         if i > 0:
-            sz[i] = total
-            over_z[i].start()
+            sz[i, h] = total
+            over_z[i, h].start()
         else:
-            mine[...] = total
+            mine[h] = total
     for i in (1, 3, 2):
-        over_z[i].wait_recv()
+        for h in range(2):
+            over_z[i, h].wait_recv()
     total = mine[...] + bz[1] + bz[2] + bz[3]
     ladder[...] = total[0].reshape(ladder.shape)
     mine[...] = total
@@ -363,7 +386,7 @@
             remote(
                 parts.at[pl.ds(0, 2)], turned.at[source, t], send_r.at[i, t], recv_r.at[i, t], rows[i - 1]
             ).wait_recv()
-    for c in copies + over_x + over_z[1:]:
+    for c in copies + list(over_x.values()) + list(over_z.values()):
         c.wait_send()
 
 
@@ -384,17 +407,17 @@
             pltpu.VMEM((4,) + chunk, jnp.float32),
             pltpu.VMEM((4,) + chunk, jnp.float32),
             pltpu.VMEM(chunk, jnp.float32),
-            dma((4,)), dma((4,)), dma((4,)), dma((4,)), dma((4, 3)), dma((4, 3)),
+            dma((4, 2)), dma((4, 2)), dma((4, 2)), dma((4, 2)), dma((4, 3)), dma((4, 3)),
         ],
         compiler_params=pltpu.CompilerParams(
-            collective_id=1, has_side_effects=True, vmem_limit_bytes=32 * 1024 * 1024
+            collective_id=1, has_side_effects=True, vmem_limit_bytes=VMEM_BYTES
         ),
     )(sums)
 
 
 def shards_8x4(amplitudes, integrals, slot_ab, slot_cd, live_count, pair_list):
     halo = halo_of(amplitudes)
-    sums = slot_sums(amplitudes, halo, integrals[0], slot_ab, slot_cd, live_count, pair_list, 18)
+    sums = slot_sums(halo, integrals[0], slot_ab, slot_cd, live_count, pair_list, 18)
     ladder, turned = sum_over_tile(sums)
     local_pairs = ladder.shape[2]
     grid = jnp.transpose(ladder.reshape(3, 6, local_pairs, ATS, TS), (2, 0, 3, 1, 4)).reshape(local_pairs, 24, SLAB)

time: 118 us -> 192 us (1.63)
  Pallas kernels: 109 us -> 186 us
  local copies, waits for them, and re-layouts: 8.17 us -> 4.84 us
    pallas_call x1, Pallas kernels: 61.2 us -> 151 us  [halo_of(): pl.pallas_call(functools.partial(halo_kernel, tiles), out_shape=jax.Shape...]
    pallas_call x1, Pallas kernels: 36.1 us -> 23.5 us  [sum_over_tile(): pl.pallas_call(sum_kernel, out_shape=(jax.ShapeDtypeStruct((3, 6) + chunk...]
    unnamed x12 -> x4, local copies, waits for them, and re-layouts: 5.97 us -> 0.86 us
where the time goes in v2:
time: 192 us
  Pallas kernels  186 us (97%)
  local copies, waits for them, and re-layouts  4.84 us (3%)
    pallas_call x1, Pallas kernels, halo_of(): pl.pallas_call(functools.partial(halo_kernel, tiles), out_shape=jax.Shape...  151 us
    pallas_call x1, Pallas kernels, sum_over_tile(): pl.pallas_call(sum_kernel, out_shape=(jax.ShapeDtypeStruct((3, 6) + chunk...  23.5 us
    pallas_call x1, Pallas kernels, slot_sums(): pl.pallas_call(slots_kernel, out_shape=jax.ShapeDtypeStruct((pair_count /...  11.4 us

profile of v2, /device:TPU:0, one launch (start us, length us, event | category | flops | bytes accessed | tf_op | source)
XLA Modules:
  0.0 191.8 jit_solution(6506405226030027092)
XLA Ops:
  0.0 0.0 copy-start
  0.0 150.7 %shard_map.64.halo = f32[216,64,256]{2,1,0:T(8,128)} custom-call(f32[72,64,256]{2,1,0:T(8,128)} %amp.1), custom_call_target="tpu_custom_call" | custom-call | tf_op jit(solution)/shard_map/pallas_call | solution.py:205
  151.4 0.0 copy-done
  151.4 0.7 copy.10.pairs
  152.1 11.4 %shard_map.65.sums = f32[8,2,18,8,128]{4,3,2,1,0:T(8,128)} custom-call(f32[216,64,256]{2,1,0:T(8,128)} %shard_map.64.halo, f32[64,128,256]{2,1,0:T(8,128)} %bitcast.13, s32[1,64]{1,0:T(1,128)} %ab.1, s32[1,64]{1,0:T(1,128)} %cd.1, s32[1,1]{1,0:T(1,128)S(6)} %copy.19.live, s32[64,2]{1,0:T(8,128)} %copy.10.pairs), custom_call_target="tpu_custom_call" | custom-call | tf_op jit(solution)/shard_map/pallas_call | solution.py:309
  163.5 23.5 %shard_map.66 = (f32[3,6,8,128]{3,2,1,0:T(8,128)}, f32[4,3,2,8,128]{4,3,2,1,0:T(8,128)}) custom-call(f32[8,2,18,8,128]{4,3,2,1,0:T(8,128)} %shard_map.65.sums), custom_call_target="tpu_custom_call" | custom-call | tf_op jit(solution)/shard_map/pallas_call | solution.py:397
  187.0 1.1 reshape.12
  188.0 0.4 copy.18
  188.4 0.2 reshape.13
  188.6 1.1 reshape.14
  189.8 0.6 copy.17
  190.4 0.4 reshape.15
  190.8 0.2 constant_dynamic-slice_fusion
  191.0 0.1 copy.14
  191.2 0.7 add.12
Async XLA Ops:
  0.0 151.4 %copy-start = (s32[64,2]{0,1:T(2,128)S(1)}, s32[64,2]{0,1:T(2,128)}, u32[]{:S(2)}) copy-start(s32[64,2]{0,1:T(2,128)} %param.11) | copy-start | bytes 1540

commit v3 on v2

--- a/solution.py
+++ b/solution.py
@@ -95,7 +95,7 @@
 
 MESH = pl.DeviceIdType.MESH
 CHUNK = 2
-WINDOW = 2
+WINDOW = 4
 GROUP = 8
 AHEAD = 2
 VMEM_BYTES = 56 * 1024 * 1024
@@ -114,7 +114,7 @@
     pl.semaphore_wait(barrier, len(devices))
 
 
-def halo_kernel(tiles, amp, halo, send, rx, rz, ry, rc, own_sem):
+def halo_kernel(tiles, amp, halo, send, rx, rz, ry, rc):
     k, r, z, x = place()
     y, core = r // 2, r % 2
     sixth = tiles // 6
@@ -165,8 +165,6 @@
 
     for j in range(WINDOW):
         go(copy_x(j))
-    own = pltpu.make_async_copy(amp, halo.at[pl.ds(2 * tiles, tiles)], own_sem)
-    own.start()
     lag = 1
     for i in range(count + 3 * lag):
         if i < count:
@@ -196,7 +194,6 @@
             copy_c(side, j).wait_recv()
     for copy in sends:
         copy.wait_send()
-    own.wait()
 
 
 def halo_of(amplitudes):
@@ -204,7 +201,7 @@
     count = tiles // 3 // CHUNK
     return pl.pallas_call(
         functools.partial(halo_kernel, tiles),
-        out_shape=jax.ShapeDtypeStruct((3 * tiles,) + amplitudes.shape[1:], jnp.float32),
+        out_shape=jax.ShapeDtypeStruct((2 * tiles,) + amplitudes.shape[1:], jnp.float32),
         in_specs=[pl.BlockSpec(memory_space=pl.ANY)],
         out_specs=pl.BlockSpec(memory_space=pl.ANY),
         scratch_shapes=[
@@ -213,7 +210,6 @@
             pltpu.SemaphoreType.DMA((count,)),
             pltpu.SemaphoreType.DMA((2, count // 2)),
             pltpu.SemaphoreType.DMA((2, count + count // 2)),
-            pltpu.SemaphoreType.DMA,
         ],
         compiler_params=pltpu.CompilerParams(
             collective_id=0, has_side_effects=True, vmem_limit_bytes=VMEM_BYTES
@@ -227,9 +223,9 @@
     return jnp.concatenate([high, low], axis=0)
 
 
-def slots_kernel(halo, blocks, ab, cd, live, pairs, out, abuf, bbuf, asem, bsem, table):
+def slots_kernel(amp, halo, blocks, ab, cd, live, pairs, out, abuf, bbuf, asem, bsem, table):
     k = lax.axis_index("tile")
-    tiles = halo.shape[0] // 3
+    tiles = amp.shape[0]
     pair_count = halo.shape[1]
     width = blocks.shape[1]
     groups = (live[0, 0] + GROUP - 1) // GROUP
@@ -248,8 +244,16 @@
             c = cd[0, s]
             mine = (c >= k * tiles) & (c < (k + 1) * tiles)
             beside = (c >= other_x * tiles) & (c < (other_x + 1) * tiles)
-            shift = jnp.where(mine, 2 - k, jnp.where(beside, -other_x, 1 - next_z))
-            pltpu.make_async_copy(halo.at[c + shift * tiles], abuf.at[s], asem.at[g]).start()
+            shift = jnp.where(beside, -other_x, 1 - next_z)
+
+            @pl.when(mine)
+            def _():
+                pltpu.make_async_copy(amp.at[c - k * tiles], abuf.at[s], asem.at[g]).start()
+
+            @pl.when(jnp.logical_not(mine))
+            def _():
+                pltpu.make_async_copy(halo.at[c + shift * tiles], abuf.at[s], asem.at[g]).start()
+
 
     def start_blocks(g, carry):
         block_copy(g).start()
@@ -301,7 +305,7 @@
     lax.fori_loop(0, pair_count, turn, 0)
 
 
-def slot_sums(halo, blocks, ab, cd, live, pair_list, tiles_ab):
+def slot_sums(amplitudes, halo, blocks, ab, cd, live, pair_list, tiles_ab):
     pair_count, depth = halo.shape[1:]
     slots, width = blocks.shape[:2]
     anywhere = pl.BlockSpec(memory_space=pl.ANY)
@@ -309,7 +313,7 @@
     return pl.pallas_call(
         slots_kernel,
         out_shape=jax.ShapeDtypeStruct((pair_count // 8, 2, tiles_ab, 8, width), jnp.float32),
-        in_specs=[anywhere] * 2 + [scalars] * 4,
+        in_specs=[anywhere] * 3 + [scalars] * 4,
         out_specs=pl.BlockSpec(memory_space=pltpu.VMEM),
         scratch_shapes=[
             pltpu.VMEM((slots, pair_count, depth), jnp.float32),
@@ -319,7 +323,7 @@
             pltpu.SMEM((128 * 128,), jnp.int32),
         ],
         compiler_params=pltpu.CompilerParams(vmem_limit_bytes=VMEM_BYTES),
-    )(halo, blocks, ab, cd, live, pair_list)
+    )(amplitudes, halo, blocks, ab, cd, live, pair_list)
 
 
 def sum_kernel(sums, ladder, turned, bx, sz, bz, mine, send_x, recv_x, send_z, recv_z, send_r, recv_r):
@@ -410,14 +414,14 @@
             dma((4, 2)), dma((4, 2)), dma((4, 2)), dma((4, 2)), dma((4, 3)), dma((4, 3)),
         ],
         compiler_params=pltpu.CompilerParams(
-            collective_id=1, has_side_effects=True, vmem_limit_bytes=VMEM_BYTES
+            collective_id=1, has_side_effects=True, vmem_limit_bytes=16 * 1024 * 1024
         ),
     )(sums)
 
 
 def shards_8x4(amplitudes, integrals, slot_ab, slot_cd, live_count, pair_list):
     halo = halo_of(amplitudes)
-    sums = slot_sums(halo, integrals[0], slot_ab, slot_cd, live_count, pair_list, 18)
+    sums = slot_sums(amplitudes, halo, integrals[0], slot_ab, slot_cd, live_count, pair_list, 18)
     ladder, turned = sum_over_tile(sums)
     local_pairs = ladder.shape[2]
     grid = jnp.transpose(ladder.reshape(3, 6, local_pairs, ATS, TS), (2, 0, 3, 1, 4)).reshape(local_pairs, 24, SLAB)

time: 192 us -> 101 us (0.53)
  Pallas kernels: 186 us -> 94.8 us
    pallas_call x1, Pallas kernels: 151 us -> 61.1 us  [halo_of(): pl.pallas_call(functools.partial(halo_kernel, tiles), out_shape=jax.Shape...]
where the time goes in v3:
time: 101 us
  Pallas kernels  94.8 us (94%)
  local copies, waits for them, and re-layouts  4.33 us (4%)
    pallas_call x1, Pallas kernels, halo_of(): pl.pallas_call(functools.partial(halo_kernel, tiles), out_shape=jax.Shape...  61.1 us
    pallas_call x1, Pallas kernels, sum_over_tile(): pl.pallas_call(sum_kernel, out_shape=(jax.ShapeDtypeStruct((3, 6) + chunk...  22.3 us
    pallas_call x1, Pallas kernels, slot_sums(): pl.pallas_call(slots_kernel, out_shape=jax.ShapeDtypeStruct((pair_count /...  11.4 us
    unnamed x6, local copies, waits for them, and re-layouts  2.12 us

profile of v3, /device:TPU:0, one launch (start us, length us, event | category | flops | bytes accessed | tf_op | source)
XLA Modules:
  0.0 100.5 jit_solution(9987697555355969190)
XLA Ops:
  0.0 0.0 copy-start.1
  0.0 61.1 %shard_map.64.halo = f32[144,64,256]{2,1,0:T(8,128)} custom-call(f32[72,64,256]{2,1,0:T(8,128)} %amp.3), custom_call_target="tpu_custom_call" | custom-call | tf_op jit(solution)/shard_map/pallas_call | solution.py:202
  61.8 0.0 copy-done.1
  61.8 0.7 copy.10.pairs
  62.5 11.4 %shard_map.65.sums = f32[8,2,18,8,128]{4,3,2,1,0:T(8,128)} custom-call(f32[72,64,256]{2,1,0:T(8,128)} %amp.3, f32[144,64,256]{2,1,0:T(8,128)} %shard_map.64.halo, f32[64,128,256]{2,1,0:T(8,128)} %bitcast.13, s32[1,64]{1,0:T(1,128)} %ab.1, s32[1,64]{1,0:T(1,128)} %cd.1, s32[1,1]{1,0:T(1,128)S(6)} %copy.19.live, s32[64,2]{1,0:T(8,128)} %copy.10.pairs), custom_call_target="tpu_custom_call" | custom-call | tf_op jit(solution)/shard_map/pallas_call | solution.py:313
  73.9 0.0 copy-start
  73.9 1.3 %copy-done = f32[8,2,18,8,128]{4,3,2,1,0:T(8,128)S(1)} copy-done((f32[8,2,18,8,128]{4,3,2,1,0:T(8,128)S(1)}, f32[8,2,18,8,128]{4,3,2,1,0:T(8,128)}, u32[]{:S(2)}) %copy-start) | copy-done | bytes 1179672
  75.2 22.3 %shard_map.66 = (f32[3,6,8,128]{3,2,1,0:T(8,128)S(1)}, f32[4,3,2,8,128]{4,3,2,1,0:T(8,128)S(1)}) custom-call(f32[8,2,18,8,128]{4,3,2,1,0:T(8,128)S(1)} %copy-done), custom_call_target="tpu_custom_call" | custom-call | tf_op jit(solution)/shard_map/pallas_call | solution.py:401
  97.5 0.2 reshape.12
  97.7 0.4 copy.18
  98.0 0.2 reshape.13
  98.2 0.2 reshape.14
  98.5 0.6 copy.17
  99.1 0.4 reshape.15
  99.6 0.2 constant_dynamic-slice_fusion
  99.7 0.1 copy.14
  99.9 0.7 add.12
Async XLA Ops:
  0.0 61.8 %copy-start.1 = (s32[64,2]{0,1:T(2,128)S(1)}, s32[64,2]{0,1:T(2,128)}, u32[]{:S(2)}) copy-start(s32[64,2]{0,1:T(2,128)} %param.11) | copy-start | bytes 1540
  73.9 1.3 %copy-start = (f32[8,2,18,8,128]{4,3,2,1,0:T(8,128)S(1)}, f32[8,2,18,8,128]{4,3,2,1,0:T(8,128)}, u32[]{:S(2)}) copy-start(f32[8,2,18,8,128]{4,3,2,1,0:T(8,128)} %shard_map.65.sums) | copy-start | bytes 3538948

commit v4 on v3

--- a/solution.py
+++ b/solution.py
@@ -203,7 +203,7 @@
         functools.partial(halo_kernel, tiles),
         out_shape=jax.ShapeDtypeStruct((2 * tiles,) + amplitudes.shape[1:], jnp.float32),
         in_specs=[pl.BlockSpec(memory_space=pl.ANY)],
-        out_specs=pl.BlockSpec(memory_space=pl.ANY),
+        out_specs=pl.BlockSpec(memory_space=pltpu.VMEM),
         scratch_shapes=[
             pltpu.SemaphoreType.DMA((6, count + count // 2)),
             pltpu.SemaphoreType.DMA((count,)),

time: 101 us -> 101 us (level)
    pallas_call x1, Pallas kernels: 11.4 us -> 7.17 us  [slot_sums(): pl.pallas_call(slots_kernel, out_shape=jax.ShapeDtypeStruct((pair_count /...]
    pallas_call x1, Pallas kernels: 61.1 us -> 63.3 us  [halo_of(): pl.pallas_call(functools.partial(halo_kernel, tiles), out_shape=jax.Shape...]
    pallas_call x1, Pallas kernels: 22.3 us -> 23.7 us  [sum_over_tile(): pl.pallas_call(sum_kernel, out_shape=(jax.ShapeDtypeStruct((3, 6) + chunk...]
where the time goes in v4:
time: 101 us; the launch traced here: 99.9 us
  Pallas kernels  94.1 us (93%)
  local copies, waits for them, and re-layouts  4.33 us (4%)
    pallas_call x1, Pallas kernels, halo_of(): pl.pallas_call(functools.partial(halo_kernel, tiles), out_shape=jax.Shape...  63.3 us
    pallas_call x1, Pallas kernels, sum_over_tile(): pl.pallas_call(sum_kernel, out_shape=(jax.ShapeDtypeStruct((3, 6) + chunk...  23.7 us
    pallas_call x1, Pallas kernels, slot_sums(): pl.pallas_call(slots_kernel, out_shape=jax.ShapeDtypeStruct((pair_count /...  7.17 us
    unnamed x6, local copies, waits for them, and re-layouts  2.12 us

profile of v4, /device:TPU:0, one launch (start us, length us, event | category | flops | bytes accessed | tf_op | source)
XLA Modules:
  0.0 99.9 jit_solution(16582767635776530023)
XLA Ops:
  0.0 0.0 copy-start.1
  0.0 63.3 %shard_map.64.halo = f32[144,64,256]{2,1,0:T(8,128)} custom-call(f32[72,64,256]{2,1,0:T(8,128)} %amp.3), custom_call_target="tpu_custom_call" | custom-call | tf_op jit(solution)/shard_map/pallas_call | solution.py:202
  64.0 0.0 copy-done.1
  64.0 0.7 copy.10.pairs
  64.7 7.2 %shard_map.65.sums = f32[8,2,18,8,128]{4,3,2,1,0:T(8,128)} custom-call(f32[72,64,256]{2,1,0:T(8,128)} %amp.3, f32[144,64,256]{2,1,0:T(8,128)} %shard_map.64.halo, f32[64,128,256]{2,1,0:T(8,128)} %bitcast.13, s32[1,64]{1,0:T(1,128)} %ab.1, s32[1,64]{1,0:T(1,128)} %cd.1, s32[1,1]{1,0:T(1,128)S(6)} %copy.19.live, s32[64,2]{1,0:T(8,128)} %copy.10.pairs), custom_call_target="tpu_custom_call" | custom-call | tf_op jit(solution)/shard_map/pallas_call | solution.py:313
  71.8 0.0 copy-start
  71.9 1.3 %copy-done = f32[8,2,18,8,128]{4,3,2,1,0:T(8,128)S(1)} copy-done((f32[8,2,18,8,128]{4,3,2,1,0:T(8,128)S(1)}, f32[8,2,18,8,128]{4,3,2,1,0:T(8,128)}, u32[]{:S(2)}) %copy-start) | copy-done | bytes 1179672
  73.1 23.7 %shard_map.66 = (f32[3,6,8,128]{3,2,1,0:T(8,128)S(1)}, f32[4,3,2,8,128]{4,3,2,1,0:T(8,128)S(1)}) custom-call(f32[8,2,18,8,128]{4,3,2,1,0:T(8,128)S(1)} %copy-done), custom_call_target="tpu_custom_call" | custom-call | tf_op jit(solution)/shard_map/pallas_call | solution.py:401
  96.8 0.2 reshape.12
  97.0 0.4 copy.18
  97.4 0.2 reshape.13
  97.6 0.2 reshape.14
  97.8 0.6 copy.17
  98.4 0.4 reshape.15
  98.9 0.2 constant_dynamic-slice_fusion
  99.1 0.1 copy.14
  99.2 0.7 add.12
Async XLA Ops:
  0.0 64.0 %copy-start.1 = (s32[64,2]{0,1:T(2,128)S(1)}, s32[64,2]{0,1:T(2,128)}, u32[]{:S(2)}) copy-start(s32[64,2]{0,1:T(2,128)} %param.11) | copy-start | bytes 1540
  71.8 1.3 %copy-start = (f32[8,2,18,8,128]{4,3,2,1,0:T(8,128)S(1)}, f32[8,2,18,8,128]{4,3,2,1,0:T(8,128)}, u32[]{:S(2)}) copy-start(f32[8,2,18,8,128]{4,3,2,1,0:T(8,128)} %shard_map.65.sums) | copy-start | bytes 3538948

commit v5 on v3

--- a/solution.py
+++ b/solution.py
@@ -98,7 +98,6 @@
 WINDOW = 4
 GROUP = 8
 AHEAD = 2
-VMEM_BYTES = 56 * 1024 * 1024
 
 
 def place():
@@ -212,7 +211,7 @@
             pltpu.SemaphoreType.DMA((2, count + count // 2)),
         ],
         compiler_params=pltpu.CompilerParams(
-            collective_id=0, has_side_effects=True, vmem_limit_bytes=VMEM_BYTES
+            collective_id=0, has_side_effects=True, vmem_limit_bytes=1024 * 1024
         ),
     )(amplitudes)
 
@@ -297,12 +296,13 @@
 
     lax.fori_loop(0, groups, step, 0)
 
-    def turn(p, carry):
-        m = table[pairs[p, 1] * 128 + pairs[p, 0]]
-        out[p // 8, 1, :, pl.ds(p % 8, 1), :] = out[m // 8, 0, :, pl.ds(m % 8, 1), :]
+    def turn(q, carry):
+        for i in range(8):
+            m = table[pairs[q * 8 + i, 1] * 128 + pairs[q * 8 + i, 0]]
+            out[q, 1, :, i : i + 1, :] = out[m // 8, 0, :, pl.ds(m % 8, 1), :]
         return carry
 
-    lax.fori_loop(0, pair_count, turn, 0)
+    lax.fori_loop(0, pair_count // 8, turn, 0)
 
 
 def slot_sums(amplitudes, halo, blocks, ab, cd, live, pair_list, tiles_ab):
@@ -322,7 +322,7 @@
             pltpu.SemaphoreType.DMA((slots // GROUP,)),
             pltpu.SMEM((128 * 128,), jnp.int32),
         ],
-        compiler_params=pltpu.CompilerParams(vmem_limit_bytes=VMEM_BYTES),
+        compiler_params=pltpu.CompilerParams(vmem_limit_bytes=24 * 1024 * 1024),
     )(amplitudes, halo, blocks, ab, cd, live, pair_list)
 
 

time: 101 us -> 114 us (1.13)
  local copies, waits for them, and re-layouts: 4.33 us -> 17.8 us
    unnamed x6 -> x18, local copies, waits for them, and re-layouts: 2.12 us -> 15.6 us
    pallas_call x1, Pallas kernels: 22.3 us -> 28.8 us  [sum_over_tile(): pl.pallas_call(sum_kernel, out_shape=(jax.ShapeDtypeStruct((3, 6) + chunk...]
    pallas_call x1, Pallas kernels: 11.4 us -> 6.86 us  [slot_sums(): pl.pallas_call(slots_kernel, out_shape=jax.ShapeDtypeStruct((pair_count /...]
    pallas_call x1, Pallas kernels: 61.1 us -> 59.5 us  [halo_of(): pl.pallas_call(functools.partial(halo_kernel, tiles), out_shape=jax.Shape...]
where the time goes in v5:
time: 114 us
  Pallas kernels  95.1 us (83%)
  local copies, waits for them, and re-layouts  17.8 us (16%)
    pallas_call x1, Pallas kernels, halo_of(): pl.pallas_call(functools.partial(halo_kernel, tiles), out_shape=jax.Shape...  59.5 us
    pallas_call x1, Pallas kernels, sum_over_tile(): pl.pallas_call(sum_kernel, out_shape=(jax.ShapeDtypeStruct((3, 6) + chunk...  28.8 us
    unnamed x18, local copies, waits for them, and re-layouts  15.6 us
    pallas_call x1, Pallas kernels, slot_sums(): pl.pallas_call(slots_kernel, out_shape=jax.ShapeDtypeStruct((pair_count /...  6.86 us

profile of v5, /device:TPU:0, one launch (start us, length us, event | category | flops | bytes accessed | tf_op | source)
XLA Modules:
  0.0 114.4 jit_solution(8086661257765198596)
XLA Ops:
  0.0 0.0 copy-start.2
  0.0 2.3 %copy-done.2 = f32[72,64,256]{2,1,0:T(8,128)S(1)} copy-done((f32[72,64,256]{2,1,0:T(8,128)S(1)}, f32[72,64,256]{2,1,0:T(8,128)}, u32[]{:S(2)}) %copy-start.2) | copy-done | bytes 4718616
  2.3 59.5 %shard_map.64.halo = f32[144,64,256]{2,1,0:T(8,128)S(1)} custom-call(f32[72,64,256]{2,1,0:T(8,128)S(1)} %copy-done.2), custom_call_target="tpu_custom_call" | custom-call | tf_op jit(solution)/shard_map/pallas_call | solution.py:201
  61.8 0.0 copy-start
  61.8 3.6 %copy-done = f32[144,64,256]{2,1,0:T(8,128)} copy-done((f32[144,64,256]{2,1,0:T(8,128)}, f32[144,64,256]{2,1,0:T(8,128)S(1)}, u32[]{:S(2)}) %copy-start) | copy-done | bytes 9437208
  66.1 0.0 copy-done.7
  66.1 0.1 copy.10.pairs
  66.2 0.0 copy-done.5
  66.2 0.0 copy-done.6
  66.2 0.0 copy-start.1
  66.2 3.7 %copy-done.1 = f32[144,64,256]{2,1,0:T(8,128)S(1)} copy-done((f32[144,64,256]{2,1,0:T(8,128)S(1)}, f32[144,64,256]{2,1,0:T(8,128)}, u32[]{:S(2)}) %copy-start.1) | copy-done | bytes 9437208
  69.9 2.3 %copy-done.3 = f32[72,64,256]{2,1,0:T(8,128)S(1)} copy-done((f32[72,64,256]{2,1,0:T(8,128)S(1)}, f32[72,64,256]{2,1,0:T(8,128)}, u32[]{:S(2)}) %copy-start.3) | copy-done | bytes 4718616
  72.2 3.4 %copy-done.4 = f32[1,64,128,256]{3,2,1,0:T(8,128)S(1)} copy-done((f32[1,64,128,256]{3,2,1,0:T(8,128)S(1)}, f32[1,64,128,256]{3,2,1,0:T(8,128)}, u32[]{:S(2)}) %copy-start.4) | copy-done | bytes 8388632
  75.6 6.9 %shard_map.65.sums = f32[8,2,18,8,128]{4,3,2,1,0:T(8,128)S(1)} custom-call(f32[72,64,256]{2,1,0:T(8,128)S(1)} %copy-done.3, f32[144,64,256]{2,1,0:T(8,128)S(1)} %copy-done.1, f32[64,128,256]{2,1,0:T(8,128)S(1)} %bitcast.13, s32[1,64]{1,0:T(1,128)S(1)} %copy-done.5, s32[1,64]{1,0:T(1,128)S(1)} %copy-done.6, s32[1,1]{1,0:T(1,128)S(6)} %copy.19.live, ...), custom_call_target="tpu_custom_call" | custom-call | tf_op jit(solution)/shard_map/pallas_call | solution.py:313
  82.5 28.8 %shard_map.66 = (f32[3,6,8,128]{3,2,1,0:T(8,128)S(1)}, f32[4,3,2,8,128]{4,3,2,1,0:T(8,128)S(1)}) custom-call(f32[8,2,18,8,128]{4,3,2,1,0:T(8,128)S(1)} %shard_map.65.sums), custom_call_target="tpu_custom_call" | custom-call | tf_op jit(solution)/shard_map/pallas_call | solution.py:401
  111.3 0.2 reshape.12
  111.5 0.4 copy.18
  111.9 0.2 reshape.13
  112.1 0.2 reshape.14
  112.3 0.6 copy.17
  112.9 0.4 reshape.15
  113.4 0.2 constant_dynamic-slice_fusion
  113.6 0.1 copy.14
  113.7 0.7 add.12
  (5 shorter events, 0.0 us)
Async XLA Ops:
  0.0 2.3 %copy-start.2 = (f32[72,64,256]{2,1,0:T(8,128)S(1)}, f32[72,64,256]{2,1,0:T(8,128)}, u32[]{:S(2)}) copy-start(f32[72,64,256]{2,1,0:T(8,128)} %amp.3) | copy-start | bytes 14155780
  2.3 63.8 %copy-start.7 = (s32[64,2]{0,1:T(2,128)S(1)}, s32[64,2]{0,1:T(2,128)}, u32[]{:S(2)}) copy-start(s32[64,2]{0,1:T(2,128)} %param.11) | copy-start | bytes 1540
  2.3 63.9 %copy-start.5 = (s32[1,64]{1,0:T(1,128)S(1)}, s32[1,64]{1,0:T(1,128)}, u32[]{:S(2)}) copy-start(s32[1,64]{1,0:T(1,128)} %ab.1) | copy-start | bytes 772
  2.3 63.9 %copy-start.6 = (s32[1,64]{1,0:T(1,128)S(1)}, s32[1,64]{1,0:T(1,128)}, u32[]{:S(2)}) copy-start(s32[1,64]{1,0:T(1,128)} %cd.1) | copy-start | bytes 772
  61.8 3.6 %copy-start = (f32[144,64,256]{2,1,0:T(8,128)}, f32[144,64,256]{2,1,0:T(8,128)S(1)}, u32[]{:S(2)}) copy-start(f32[144,64,256]{2,1,0:T(8,128)S(1)} %shard_map.64.halo) | copy-start | bytes 28311556
  66.2 3.7 %copy-start.1 = (f32[144,64,256]{2,1,0:T(8,128)S(1)}, f32[144,64,256]{2,1,0:T(8,128)}, u32[]{:S(2)}) copy-start(f32[144,64,256]{2,1,0:T(8,128)} %copy-done) | copy-start | bytes 28311556
  69.9 2.3 %copy-start.3 = (f32[72,64,256]{2,1,0:T(8,128)S(1)}, f32[72,64,256]{2,1,0:T(8,128)}, u32[]{:S(2)}) copy-start(f32[72,64,256]{2,1,0:T(8,128)} %amp.3) | copy-start | bytes 14155780
  72.2 3.4 %copy-start.4 = (f32[1,64,128,256]{3,2,1,0:T(8,128)S(1)}, f32[1,64,128,256]{3,2,1,0:T(8,128)}, u32[]{:S(2)}) copy-start(f32[1,64,128,256]{3,2,1,0:T(8,128)} %param.7) | copy-start | bytes 25165828

commit v6 on v5

--- a/solution.py
+++ b/solution.py
@@ -98,6 +98,7 @@
 WINDOW = 4
 GROUP = 8
 AHEAD = 2
+VMEM_BYTES = 56 * 1024 * 1024
 
 
 def place():
@@ -211,7 +212,7 @@
             pltpu.SemaphoreType.DMA((2, count + count // 2)),
         ],
         compiler_params=pltpu.CompilerParams(
-            collective_id=0, has_side_effects=True, vmem_limit_bytes=1024 * 1024
+            collective_id=0, has_side_effects=True, vmem_limit_bytes=VMEM_BYTES
         ),
     )(amplitudes)
 
@@ -322,7 +323,7 @@
             pltpu.SemaphoreType.DMA((slots // GROUP,)),
             pltpu.SMEM((128 * 128,), jnp.int32),
         ],
-        compiler_params=pltpu.CompilerParams(vmem_limit_bytes=24 * 1024 * 1024),
+        compiler_params=pltpu.CompilerParams(vmem_limit_bytes=VMEM_BYTES),
     )(amplitudes, halo, blocks, ab, cd, live, pair_list)
 
 
@@ -338,7 +339,7 @@
             src_ref=src, dst_ref=dst, send_sem=sent, recv_sem=received, device_id=device, device_id_type=MESH
         )
 
-    steps = [(i, h) for i in (2, 1, 3, 0) for h in range(2)]
+    steps = [(i, h) for h in (1, 0) for i in (2, 1, 3, 0)]
     over_x = {
         (i, h): remote(
             sums.at[(z + i) % 4 * 2 + 1 - x, h], bx.at[i, h], send_x.at[i, h], recv_x.at[i, h], other_x
@@ -361,12 +362,12 @@
             over_z[i, h].start()
         else:
             mine[h] = total
-    for i in (1, 3, 2):
-        for h in range(2):
+    def finish(h):
+        for i in (1, 3, 2):
             over_z[i, h].wait_recv()
-    total = mine[...] + bz[1] + bz[2] + bz[3]
-    ladder[...] = total[0].reshape(ladder.shape)
-    mine[...] = total
+        return mine[h] + bz[1, h] + bz[2, h] + bz[3, h]
+
+    mine[1] = finish(1)
     parts = mine.at[1]
 
     def over_row(i):
@@ -384,6 +385,7 @@
     own = r * 3 // 2
     for t in range(3):
         turned[r, t] = mine[1, pl.ds(t * 6 + own, 2)]
+    ladder[...] = finish(0).reshape(ladder.shape)
     for i in range(1, 4):
         source = (r + 4 - i) % 4
         for t in range(3):

time: 114 us -> 96.6 us (0.85)
  local copies, waits for them, and re-layouts: 17.8 us -> 4.33 us
  Pallas kernels: 95.1 us -> 91.2 us
    unnamed x18 -> x6, local copies, waits for them, and re-layouts: 15.6 us -> 2.12 us
    pallas_call x1, Pallas kernels: 28.8 us -> 24.4 us  [sum_over_tile(): pl.pallas_call(sum_kernel, out_shape=(jax.ShapeDtypeStruct((3, 6) + chunk...]
    pallas_call x1, Pallas kernels: 59.5 us -> 61.1 us  [halo_of(): pl.pallas_call(functools.partial(halo_kernel, tiles), out_shape=jax.Shape...]
    pallas_call x1, Pallas kernels: 6.86 us -> 5.66 us  [slot_sums(): pl.pallas_call(slots_kernel, out_shape=jax.ShapeDtypeStruct((pair_count /...]
where the time goes in v6:
time: 96.6 us; the launch traced here: 96.9 us
  Pallas kernels  91.2 us (94%)
  local copies, waits for them, and re-layouts  4.33 us (4%)
    pallas_call x1, Pallas kernels, halo_of(): pl.pallas_call(functools.partial(halo_kernel, tiles), out_shape=jax.Shape...  61.1 us
    pallas_call x1, Pallas kernels, sum_over_tile(): pl.pallas_call(sum_kernel, out_shape=(jax.ShapeDtypeStruct((3, 6) + chunk...  24.4 us
    pallas_call x1, Pallas kernels, slot_sums(): pl.pallas_call(slots_kernel, out_shape=jax.ShapeDtypeStruct((pair_count /...  5.66 us
    unnamed x6, local copies, waits for them, and re-layouts  2.12 us

profile of v6, /device:TPU:0, one launch (start us, length us, event | category | flops | bytes accessed | tf_op | source)
XLA Modules:
  0.0 96.9 jit_solution(11292647197618161181)
XLA Ops:
  0.0 0.0 copy-start.1
  0.0 61.1 %shard_map.64.halo = f32[144,64,256]{2,1,0:T(8,128)} custom-call(f32[72,64,256]{2,1,0:T(8,128)} %amp.3), custom_call_target="tpu_custom_call" | custom-call | tf_op jit(solution)/shard_map/pallas_call | solution.py:202
  61.8 0.0 copy-done.1
  61.8 0.7 copy.10.pairs
  62.5 5.7 %shard_map.65.sums = f32[8,2,18,8,128]{4,3,2,1,0:T(8,128)} custom-call(f32[72,64,256]{2,1,0:T(8,128)} %amp.3, f32[144,64,256]{2,1,0:T(8,128)} %shard_map.64.halo, f32[64,128,256]{2,1,0:T(8,128)} %bitcast.13, s32[1,64]{1,0:T(1,128)} %ab.1, s32[1,64]{1,0:T(1,128)} %cd.1, s32[1,1]{1,0:T(1,128)S(6)} %copy.19.live, s32[64,2]{1,0:T(8,128)} %copy.10.pairs), custom_call_target="tpu_custom_call" | custom-call | tf_op jit(solution)/shard_map/pallas_call | solution.py:314
  68.1 0.0 copy-start
  68.2 1.3 %copy-done = f32[8,2,18,8,128]{4,3,2,1,0:T(8,128)S(1)} copy-done((f32[8,2,18,8,128]{4,3,2,1,0:T(8,128)S(1)}, f32[8,2,18,8,128]{4,3,2,1,0:T(8,128)}, u32[]{:S(2)}) %copy-start) | copy-done | bytes 1179672
  69.4 24.4 %shard_map.66 = (f32[3,6,8,128]{3,2,1,0:T(8,128)S(1)}, f32[4,3,2,8,128]{4,3,2,1,0:T(8,128)S(1)}) custom-call(f32[8,2,18,8,128]{4,3,2,1,0:T(8,128)S(1)} %copy-done), custom_call_target="tpu_custom_call" | custom-call | tf_op jit(solution)/shard_map/pallas_call | solution.py:403
  93.8 0.2 reshape.12
  94.0 0.4 copy.18
  94.4 0.2 reshape.13
  94.6 0.2 reshape.14
  94.9 0.6 copy.17
  95.5 0.4 reshape.15
  95.9 0.2 constant_dynamic-slice_fusion
  96.1 0.1 copy.14
  96.3 0.7 add.12
Async XLA Ops:
  0.0 61.8 %copy-start.1 = (s32[64,2]{0,1:T(2,128)S(1)}, s32[64,2]{0,1:T(2,128)}, u32[]{:S(2)}) copy-start(s32[64,2]{0,1:T(2,128)} %param.11) | copy-start | bytes 1540
  68.1 1.3 %copy-start = (f32[8,2,18,8,128]{4,3,2,1,0:T(8,128)S(1)}, f32[8,2,18,8,128]{4,3,2,1,0:T(8,128)}, u32[]{:S(2)}) copy-start(f32[8,2,18,8,128]{4,3,2,1,0:T(8,128)} %shard_map.65.sums) | copy-start | bytes 3538948

commit v7 on v6

--- a/solution.py
+++ b/solution.py
@@ -94,8 +94,8 @@
 
 
 MESH = pl.DeviceIdType.MESH
-CHUNK = 2
-WINDOW = 4
+CHUNK = 1
+WINDOW = 8
 GROUP = 8
 AHEAD = 2
 VMEM_BYTES = 56 * 1024 * 1024
@@ -165,7 +165,7 @@
 
     for j in range(WINDOW):
         go(copy_x(j))
-    lag = 1
+    lag = 2
     for i in range(count + 3 * lag):
         if i < count:
             copy_x(i).wait_recv()
@@ -267,7 +267,7 @@
     out[...] = jnp.zeros_like(out)
 
     def note(p, carry):
-        table[pairs[p, 0] * 128 + pairs[p, 1]] = p
+        table[pairs[0, p] * 128 + pairs[1, p]] = p
         return carry
 
     lax.fori_loop(0, pair_count, note, 0)
@@ -299,7 +299,7 @@
 
     def turn(q, carry):
         for i in range(8):
-            m = table[pairs[q * 8 + i, 1] * 128 + pairs[q * 8 + i, 0]]
+            m = table[pairs[1, q * 8 + i] * 128 + pairs[0, q * 8 + i]]
             out[q, 1, :, i : i + 1, :] = out[m // 8, 0, :, pl.ds(m % 8, 1), :]
         return carry
 
@@ -350,12 +350,12 @@
         (i, h): remote(sz.at[i, h], bz.at[i, h], send_z.at[i, h], recv_z.at[i, h], zs[i - 1])
         for i, h in steps if i > 0
     }
-    for step in steps[:WINDOW]:
+    for step in steps[: WINDOW // 2]:
         over_x[step].start()
     for j, (i, h) in enumerate(steps):
         over_x[i, h].wait_recv()
-        if j + WINDOW < len(steps):
-            over_x[steps[j + WINDOW]].start()
+        if j + WINDOW // 2 < len(steps):
+            over_x[steps[j + WINDOW // 2]].start()
         total = bx[i, h] + sums[(z + i) % 4 * 2 + x, h]
         if i > 0:
             sz[i, h] = total
@@ -423,7 +423,7 @@
 
 def shards_8x4(amplitudes, integrals, slot_ab, slot_cd, live_count, pair_list):
     halo = halo_of(amplitudes)
-    sums = slot_sums(amplitudes, halo, integrals[0], slot_ab, slot_cd, live_count, pair_list, 18)
+    sums = slot_sums(amplitudes, halo, integrals[0], slot_ab, slot_cd, live_count, pair_list.T, 18)
     ladder, turned = sum_over_tile(sums)
     local_pairs = ladder.shape[2]
     grid = jnp.transpose(ladder.reshape(3, 6, local_pairs, ATS, TS), (2, 0, 3, 1, 4)).reshape(local_pairs, 24, SLAB)

time: 96.6 us -> 95.7 us (level)
    pallas_call x1, Pallas kernels: 24.4 us -> 23.3 us  [sum_over_tile(): pl.pallas_call(sum_kernel, out_shape=(jax.ShapeDtypeStruct((3, 6) + chunk...]
    unnamed x6 -> x3, local copies, waits for them, and re-layouts: 2.12 us -> 1.41 us
where the time goes in v7:
time: 95.7 us; the launch traced here: 96.2 us
  Pallas kernels  91.1 us (95%)
  local copies, waits for them, and re-layouts  3.62 us (4%)
    pallas_call x1, Pallas kernels, halo_of(): pl.pallas_call(functools.partial(halo_kernel, tiles), out_shape=jax.Shape...  61.9 us
    pallas_call x1, Pallas kernels, sum_over_tile(): pl.pallas_call(sum_kernel, out_shape=(jax.ShapeDtypeStruct((3, 6) + chunk...  23.3 us
    pallas_call x1, Pallas kernels, slot_sums(): pl.pallas_call(slots_kernel, out_shape=jax.ShapeDtypeStruct((pair_count /...  5.87 us

profile of v7, /device:TPU:0, one launch (start us, length us, event | category | flops | bytes accessed | tf_op | source)
XLA Modules:
  0.0 96.2 jit_solution(1062469093788575074)
XLA Ops:
  0.0 61.9 %shard_map.64.halo = f32[144,64,256]{2,1,0:T(8,128)} custom-call(f32[72,64,256]{2,1,0:T(8,128)} %amp.3), custom_call_target="tpu_custom_call" | custom-call | tf_op jit(solution)/shard_map/pallas_call | solution.py:202
  62.6 5.9 %shard_map.65.sums = f32[8,2,18,8,128]{4,3,2,1,0:T(8,128)} custom-call(f32[72,64,256]{2,1,0:T(8,128)} %amp.3, f32[144,64,256]{2,1,0:T(8,128)} %shard_map.64.halo, f32[64,128,256]{2,1,0:T(8,128)} %bitcast.14, s32[1,64]{1,0:T(1,128)} %ab.1, s32[1,64]{1,0:T(1,128)} %cd.1, s32[1,1]{1,0:T(1,128)S(6)} %copy.17.live, s32[2,64]{1,0:T(2,128)} %bitcast.17), custom_call_target="tpu_custom_call" | custom-call | tf_op jit(solution)/shard_map/pallas_call | solution.py:314
  68.5 0.0 copy-start
  68.5 1.3 %copy-done = f32[8,2,18,8,128]{4,3,2,1,0:T(8,128)S(1)} copy-done((f32[8,2,18,8,128]{4,3,2,1,0:T(8,128)S(1)}, f32[8,2,18,8,128]{4,3,2,1,0:T(8,128)}, u32[]{:S(2)}) %copy-start) | copy-done | bytes 1179672
  69.7 23.3 %shard_map.66 = (f32[3,6,8,128]{3,2,1,0:T(8,128)S(1)}, f32[4,3,2,8,128]{4,3,2,1,0:T(8,128)S(1)}) custom-call(f32[8,2,18,8,128]{4,3,2,1,0:T(8,128)S(1)} %copy-done), custom_call_target="tpu_custom_call" | custom-call | tf_op jit(solution)/shard_map/pallas_call | solution.py:403
  93.1 0.2 reshape.12
  93.3 0.4 copy.16
  93.6 0.2 reshape.13
  93.8 0.2 reshape.14
  94.1 0.6 copy.15
  94.7 0.4 reshape.15
  95.2 0.2 constant_dynamic-slice_fusion
  95.3 0.1 copy.12
  95.5 0.7 add.12
Async XLA Ops:
  68.5 1.3 %copy-start = (f32[8,2,18,8,128]{4,3,2,1,0:T(8,128)S(1)}, f32[8,2,18,8,128]{4,3,2,1,0:T(8,128)}, u32[]{:S(2)}) copy-start(f32[8,2,18,8,128]{4,3,2,1,0:T(8,128)} %shard_map.65.sums) | copy-start | bytes 3538948

commit v8 on v6

--- a/solution.py
+++ b/solution.py
@@ -94,7 +94,7 @@
 
 
 MESH = pl.DeviceIdType.MESH
-CHUNK = 2
+CHUNK = 3
 WINDOW = 4
 GROUP = 8
 AHEAD = 2
@@ -267,7 +267,7 @@
     out[...] = jnp.zeros_like(out)
 
     def note(p, carry):
-        table[pairs[p, 0] * 128 + pairs[p, 1]] = p
+        table[pairs[0, p] * 128 + pairs[1, p]] = p
         return carry
 
     lax.fori_loop(0, pair_count, note, 0)
@@ -299,7 +299,7 @@
 
     def turn(q, carry):
         for i in range(8):
-            m = table[pairs[q * 8 + i, 1] * 128 + pairs[q * 8 + i, 0]]
+            m = table[pairs[1, q * 8 + i] * 128 + pairs[0, q * 8 + i]]
             out[q, 1, :, i : i + 1, :] = out[m // 8, 0, :, pl.ds(m % 8, 1), :]
         return carry
 
@@ -423,7 +423,7 @@
 
 def shards_8x4(amplitudes, integrals, slot_ab, slot_cd, live_count, pair_list):
     halo = halo_of(amplitudes)
-    sums = slot_sums(amplitudes, halo, integrals[0], slot_ab, slot_cd, live_count, pair_list, 18)
+    sums = slot_sums(amplitudes, halo, integrals[0], slot_ab, slot_cd, live_count, pair_list.T, 18)
     ladder, turned = sum_over_tile(sums)
     local_pairs = ladder.shape[2]
     grid = jnp.transpose(ladder.reshape(3, 6, local_pairs, ATS, TS), (2, 0, 3, 1, 4)).reshape(local_pairs, 24, SLAB)

time: 96.6 us -> 90 us (0.932)
  Pallas kernels: 91.2 us -> 85.5 us
    pallas_call x1, Pallas kernels: 61.1 us -> 56.4 us  [halo_of(): pl.pallas_call(functools.partial(halo_kernel, tiles), out_shape=jax.Shape...]
    pallas_call x1, Pallas kernels: 24.4 us -> 23.2 us  [sum_over_tile(): pl.pallas_call(sum_kernel, out_shape=(jax.ShapeDtypeStruct((3, 6) + chunk...]
    unnamed x6 -> x3, local copies, waits for them, and re-layouts: 2.12 us -> 1.41 us
where the time goes in v8:
time: 90 us; the launch traced here: 90.5 us
  Pallas kernels  85.5 us (95%)
  local copies, waits for them, and re-layouts  3.62 us (4%)
    pallas_call x1, Pallas kernels, halo_of(): pl.pallas_call(functools.partial(halo_kernel, tiles), out_shape=jax.Shape...  56.4 us
    pallas_call x1, Pallas kernels, sum_over_tile(): pl.pallas_call(sum_kernel, out_shape=(jax.ShapeDtypeStruct((3, 6) + chunk...  23.2 us
    pallas_call x1, Pallas kernels, slot_sums(): pl.pallas_call(slots_kernel, out_shape=jax.ShapeDtypeStruct((pair_count /...  5.9 us

profile of v8, /device:TPU:0, one launch (start us, length us, event | category | flops | bytes accessed | tf_op | source)
XLA Modules:
  0.0 90.5 jit_solution(2011934033383240876)
XLA Ops:
  0.0 56.4 %shard_map.64.halo = f32[144,64,256]{2,1,0:T(8,128)} custom-call(f32[72,64,256]{2,1,0:T(8,128)} %amp.3), custom_call_target="tpu_custom_call" | custom-call | tf_op jit(solution)/shard_map/pallas_call | solution.py:202
  57.1 5.9 %shard_map.65.sums = f32[8,2,18,8,128]{4,3,2,1,0:T(8,128)} custom-call(f32[72,64,256]{2,1,0:T(8,128)} %amp.3, f32[144,64,256]{2,1,0:T(8,128)} %shard_map.64.halo, f32[64,128,256]{2,1,0:T(8,128)} %bitcast.14, s32[1,64]{1,0:T(1,128)} %ab.1, s32[1,64]{1,0:T(1,128)} %cd.1, s32[1,1]{1,0:T(1,128)S(6)} %copy.17.live, s32[2,64]{1,0:T(2,128)} %bitcast.17), custom_call_target="tpu_custom_call" | custom-call | tf_op jit(solution)/shard_map/pallas_call | solution.py:314
  63.0 0.0 copy-start
  63.0 1.3 %copy-done = f32[8,2,18,8,128]{4,3,2,1,0:T(8,128)S(1)} copy-done((f32[8,2,18,8,128]{4,3,2,1,0:T(8,128)S(1)}, f32[8,2,18,8,128]{4,3,2,1,0:T(8,128)}, u32[]{:S(2)}) %copy-start) | copy-done | bytes 1179672
  64.2 23.2 %shard_map.66 = (f32[3,6,8,128]{3,2,1,0:T(8,128)S(1)}, f32[4,3,2,8,128]{4,3,2,1,0:T(8,128)S(1)}) custom-call(f32[8,2,18,8,128]{4,3,2,1,0:T(8,128)S(1)} %copy-done), custom_call_target="tpu_custom_call" | custom-call | tf_op jit(solution)/shard_map/pallas_call | solution.py:403
  87.4 0.2 reshape.12
  87.6 0.4 copy.16
  88.0 0.2 reshape.13
  88.2 0.2 reshape.14
  88.5 0.6 copy.15
  89.1 0.4 reshape.15
  89.5 0.2 constant_dynamic-slice_fusion
  89.7 0.1 copy.12
  89.9 0.7 add.12
Async XLA Ops:
  63.0 1.3 %copy-start = (f32[8,2,18,8,128]{4,3,2,1,0:T(8,128)S(1)}, f32[8,2,18,8,128]{4,3,2,1,0:T(8,128)}, u32[]{:S(2)}) copy-start(f32[8,2,18,8,128]{4,3,2,1,0:T(8,128)} %shard_map.65.sums) | copy-start | bytes 3538948
